TPU v7x, 128 devices: a whole 4x4x4 slice. The times are simulated.
128 devices in a mesh: narrow: 4 (over y), wide: 32 (over z, x, core).
Axes of the slice: x: 4, y: 4, z: 4, core: 2. Of those that a mesh axis runs over, the one named last changes fastest.
Arguments:
- hidden_state: bfloat16 [256, 8192], P(('narrow', 'wide')), may hold values from -6 to 6
- query_weight: bfloat16 [8192, 8192], P('narrow', 'wide'), may hold values from -0.0625 to 0.0625
- memory_weight: bfloat16 [8192, 2, 1024], P('narrow', None, 'wide'), may hold values from -0.0625 to 0.0625
- output_weight: bfloat16 [8192, 8192], P('wide', 'narrow'), may hold values from -1 to 1
- key_cache: bfloat16 [256, 2048, 1024], P(('narrow', 'wide')), may hold values from -122 to 122
- value_cache: bfloat16 [256, 2048, 1024], P(('narrow', 'wide')), may hold values from -6 to 6
- cache_lengths: int32 [256], P(('narrow', 'wide')), may hold values from 2 to 2048, as said below
Outputs:
- attention_out: bfloat16 [256, 8192], P(('narrow', 'wide'))
Inputs may be any that keep to these rules, and one draw needn't show every extreme that they name: `cache_lengths`: each sequence's length; some sequence has exactly 2048.
All inputs are finite; a program needn't handle non-finite values.
Results may differ from a plain program's by a relative error of at most 0.022.
Values may be sent and summed in bfloat16 or wider, within the bound.
No kernel may reach another device: no remote copies, remote signals or barrier semaphores. Data moves between devices by JAX's collectives and lax.ppermute only.
A program may use at most 128 MiB of HBM per device.

v0:
```python
import math

import jax
import jax.numpy as jnp
from jax import lax
from jax.sharding import PartitionSpec as P

HD = 128


rope_base = 500000.0
masked_score = -1e30


def rotate(values, positions):
    half_width = values.shape[-1] // 2
    frequency = jnp.exp(
        -jnp.log(rope_base) * jnp.arange(half_width, dtype=jnp.float32) * 2.0 / values.shape[-1]
    )
    angles = positions.astype(jnp.float32)[:, None, None] * frequency
    cosine = jnp.cos(angles)
    sine_part = jnp.sin(angles)
    first_half = values[..., :half_width]
    second = values[..., half_width:]
    return jnp.concatenate(
        [first_half * cosine - second * sine_part, second * cosine + first_half * sine_part],
        axis=-1,
    )


def attend(rotated_queries, rotated_keys, fresh_values, key_cache, value_cache, cache_lengths):
    seq_rows, head_count, head_width = rotated_queries.shape
    group_count = rotated_keys.shape[1]
    per_group = head_count // group_count
    cache_len = key_cache.shape[1]
    block_size = min(512, cache_len)
    score_scale = 1.0 / math.sqrt(head_width)
    grouped = rotated_queries.reshape(seq_rows, group_count, per_group, head_width)
    own_score = (
        jnp.einsum("lgjd,lgd->lgj", grouped, rotated_keys, preferred_element_type=jnp.float32)
        * score_scale
    )
    denominator = jnp.ones_like(own_score)
    carried = jnp.broadcast_to(
        fresh_values.astype(jnp.float32)[:, :, None, :],
        (seq_rows, group_count, per_group, head_width),
    )
    longest = jnp.max(cache_lengths)
    amount = (longest + block_size - 1) // block_size

    def visit(block_index, carry):
        running_max, denominator, carried = carry
        offset = block_index * block_size
        key_block = lax.dynamic_slice_in_dim(key_cache, offset, block_size, 1).reshape(
            seq_rows, block_size, group_count, head_width
        )
        value_block = lax.dynamic_slice_in_dim(value_cache, offset, block_size, 1).reshape(
            seq_rows, block_size, group_count, head_width
        )
        scores = (
            jnp.einsum("lgjd,lbgd->lgjb", grouped, key_block, preferred_element_type=jnp.float32)
            * score_scale
        )
        live_mask = (offset + jnp.arange(block_size, dtype=jnp.int32))[None, :] < cache_lengths[
            :, None
        ]
        scores = jnp.where(live_mask[:, None, None, :], scores, masked_score)
        fresh_max = jnp.maximum(running_max, jnp.max(scores, axis=-1))
        weights = jnp.exp(scores - fresh_max[..., None])
        factor = jnp.exp(running_max - fresh_max)
        denominator = denominator * factor + jnp.sum(weights, axis=-1)
        carried = carried * factor[..., None] + jnp.einsum(
            "lgjb,lbgd->lgjd",
            weights.astype(jnp.bfloat16),
            value_block,
            preferred_element_type=jnp.float32,
        )
        return (fresh_max, denominator, carried)

    running_max, denominator, carried = lax.fori_loop(
        0, amount, visit, (own_score, denominator, carried)
    )
    return (
        (carried / denominator[..., None])
        .reshape(seq_rows, head_count * head_width)
        .astype(jnp.bfloat16)
    )


def on_device(
    hidden_state, query_weight, memory_weight, output_weight, key_cache, value_cache, cache_lengths
):
    narrow_count = lax.axis_size("narrow")
    wide_count = lax.axis_size("wide")
    seq_rows, model_width = hidden_state.shape
    width_part = model_width // narrow_count
    joined = jnp.concatenate(
        [query_weight, memory_weight.reshape(memory_weight.shape[0], -1)], axis=1
    )
    query_cols = query_weight.shape[1]
    memory_half = memory_weight.shape[2]
    total_cols = joined.shape[1]
    pieces = hidden_state.reshape(1, seq_rows, narrow_count, width_part)
    local_cols = lax.all_to_all(pieces, "narrow", split_axis=2, concat_axis=0, tiled=True)
    local_cols = local_cols.reshape(1, narrow_count, seq_rows, width_part)
    shard_piece = lax.all_gather(local_cols, "wide", axis=0, tiled=True)
    flattened = shard_piece.reshape(-1, width_part)
    product = jnp.dot(flattened, joined, preferred_element_type=jnp.float32)
    partial_terms = product.reshape(shard_piece.shape[0], narrow_count, seq_rows, total_cols)
    summed = lax.psum_scatter(partial_terms, "narrow", scatter_dimension=1, tiled=True)
    projected = summed.astype(jnp.bfloat16).reshape(wide_count, seq_rows, 1, total_cols)
    arranged = lax.all_to_all(projected, "wide", split_axis=0, concat_axis=2, tiled=True).reshape(
        seq_rows, wide_count, total_cols
    )
    query_flat = arranged[:, :, :query_cols].reshape(seq_rows, -1, HD)
    key_flat = arranged[:, :, query_cols : query_cols + memory_half].reshape(seq_rows, -1, HD)
    value_flat = arranged[:, :, query_cols + memory_half :].reshape(seq_rows, -1, HD)
    rotated_queries = rotate(query_flat.astype(jnp.float32), cache_lengths).astype(jnp.bfloat16)
    rotated_keys = rotate(key_flat.astype(jnp.float32), cache_lengths).astype(jnp.bfloat16)
    attended = attend(
        rotated_queries, rotated_keys, value_flat, key_cache, value_cache, cache_lengths
    )
    heads_local = output_weight.shape[0]
    spread = attended.reshape(seq_rows, wide_count, heads_local)
    returned = lax.all_to_all(spread, "wide", split_axis=1, concat_axis=0, tiled=True)
    blocks = returned.reshape(wide_count, 1, seq_rows, heads_local)
    gathered = lax.all_gather(blocks, "narrow", axis=1, tiled=True)
    product = jnp.dot(
        gathered.reshape(-1, heads_local), output_weight, preferred_element_type=jnp.float32
    )
    own_rows = lax.psum_scatter(
        product.reshape(1 * lax.axis_size("wide"), narrow_count, seq_rows, width_part).astype(
            jnp.bfloat16
        ),
        "wide",
        scatter_dimension=0,
        tiled=True,
    )
    return lax.all_to_all(own_rows, "narrow", split_axis=1, concat_axis=3, tiled=True).reshape(
        seq_rows, model_width
    )


def solution(mesh):
    in_specs = (
        P(("narrow", "wide"), None),
        P("narrow", "wide"),
        P("narrow", None, "wide"),
        P("wide", "narrow"),
        P(("narrow", "wide"), None, None),
        P(("narrow", "wide"), None, None),
        P(("narrow", "wide")),
    )
    out_specs = P(("narrow", "wide"), None)
    return jax.shard_map(
        on_device, mesh=mesh, in_specs=in_specs, out_specs=out_specs, check_vma=False
    )
```

profile of v0, /device:TPU:0, one launch (start us, length us, event | category | flops | bytes accessed | tf_op | source)
XLA Modules:
  0.0 293.2 jit_solution(16914971544459527211)
XLA Ops:
  6.5 10.2 %all_to_all.60 = bf16[1,2,4,2048]{3,1,0,2:T(2,128)(2,1)} all-to-all(bf16[1,2,4,2048]{3,1,0,2:T(2,128)(2,1)} %bitcast.77), channel_id=1, replica_groups=mesh['narrow'=4,'wide'=32] {'narrow'}, dimensions={2} | all-to-all | bytes 65536 | tf_op jit(solution)/shard_map/all_to_all | solution.py:104
  16.8 1.2 copy.48
  18.1 42.1 %all-gather.4.cloned.1.call-done = bf16[128,1,2,1,2048]{4,2,3,1,0:T(2,128)(2,1)} async-done(((bf16[4,1,2,1,2048]{4,2,3,1,0:T(2,128)(2,1)}), bf16[128,1,2,1,2048]{4,2,3,1,0:T(2,128)(2,1)}) %all-gather.4.cloned.1.call-update) | async-done | bytes 1048592 | tf_op jit(solution)/shard_map/all_gather | solution.py:106
  60.2 1.5 reshape.156
  61.6 1.8 fusion.10
  63.5 0.2 copy.50
  63.7 0.2 reshape.157
  63.9 0.8 copy.51
  64.8 0.6 fusion.21
  65.4 19.6 %reduce-scatter.2.cloned.1.call-done = f32[32,1,2,320]{3,0,2,1:T(8,128)} async-done(((f32[32,4,2,320]{3,0,2,1:T(8,128)}), f32[32,1,2,320]{3,0,2,1:T(8,128)}) %reduce-scatter.2.cloned.1.call-update) | async-done | bytes 81936 | tf_op jit(solution)/shard_map/reduce_scatter | solution.py:110
  85.0 0.9 convert_bitcast_fusion
  85.9 0.7 copy.52
  86.5 7.2 %all-to-all-start.1 = ((bf16[32,2,1,320]{3,1,2,0:T(2,128)(2,1)}), bf16[32,2,1,320]{3,1,2,0:T(2,128)(2,1)S(1)}, u32[]{:S(2)}, u32[]{:S(2)}) async-start(bf16[32,2,1,320]{3,1,2,0:T(2,128)(2,1)} %copy.52), calls=%async_computation.2 | async-start | bytes 98304 | tf_op jit(solution)/shard_map/all_to_all | solution.py:112
  94.6 6.6 %all-to-all-done.1 = bf16[32,2,1,320]{3,1,2,0:T(2,128)(2,1)S(1)} async-done(((bf16[32,2,1,320]{3,1,2,0:T(2,128)(2,1)}), bf16[32,2,1,320]{3,1,2,0:T(2,128)(2,1)S(1)}, u32[]{:S(2)}, u32[]{:S(2)}) %all-to-all-start.1) | async-done | bytes 40992 | tf_op jit(solution)/shard_map/all_to_all | solution.py:112
  101.7 0.1 fusion.17
  102.0 11.8 %while.14 = (s32[]{:T(128)}, f32[2,8,8]{2,1,0:T(8,128)S(1)}, f32[2,8,8]{2,1,0:T(8,128)S(1)}, f32[2,8,8,128]{3,2,1,0:T(8,128)S(1)}, s32[]{:T(128)}, /*index=5*/s3...) while((s32[]{:T(128)}, f32[2,8,8]{2,1,0:T(8,128)S(1)}, ...), condition=%wide.region_5.6_spmd, body=%wide.region_2.5_spmd.sunk | while | flops 34047748 | bytes 21936316 | solution.py:80
  102.0 4.6 %constant_dynamic-slice_fusion.4 = (bf16[2,512,1024]{2,1,0:T(8,128)(2,1)}, bf16[2,512,1024]{2,1,0:T(8,128)(2,1)}) fusion(bf16[2,2048,1024]{2,1,0:T(8,128)(2,1)} %get-tuple-element.228, s32[]{:T(128)S(6)} %select_n.21, bf16[2,2048,1024]{2,1,0:T(8,128)(2,1)} %get-tuple-element.226), kind=kLoop, calls=%fused_computation.12.clone.1 | loop fusion | bytes 8388612 | tf_op jit(solution)/shard_map/while/body/dynamic_slice | solution.py:57
  106.6 2.9 copy.73
  109.6 0.5 fusion.37
  110.0 0.2 fusion.38
  110.2 2.9 copy.74
  113.1 0.7 convolution_add_fusion.2
  113.8 0.1 divide_convert_fusion
  114.0 45.6 %all_to_all.61 = bf16[2,32,256]{2,0,1:T(2,128)(2,1)S(1)} all-to-all(bf16[2,32,256]{2,0,1:T(2,128)(2,1)S(1)} %copy.56), channel_id=1, replica_groups=mesh['narrow'=4,'wide'=32] {'wide'}, dimensions={1} | all-to-all | bytes 65536 | tf_op jit(solution)/shard_map/all_to_all | solution.py:125
  159.5 12.0 %all-gather.1 = bf16[32,8,1,256]{3,0,2,1:T(8,128)(2,1)S(1)} all-gather(bf16[32,2,1,256]{3,0,2,1:T(8,128)(2,1)S(1)} %copy.57), channel_id=3, replica_groups=mesh['narrow'=4,'wide'=32] {'narrow'}, dimensions={1}, use_global_device_ids=true | all-gather | bytes 163840 | tf_op jit(solution)/shard_map/all_gather | solution.py:127
  171.6 0.4 convolution_convert_fusion
  172.0 1.8 copy.58
  173.9 0.6 dynamic-slice
  174.5 100.5 %all-reduce.3.cloned.1.call-done = bf16[32,4,2,2048]{3,1,2,0:T(4,128)(2,1)} async-done(((bf16[32,4,2,2048]{3,1,2,0:T(4,128)(2,1)}), bf16[32,4,2,2048]{3,1,2,0:T(4,128)(2,1)}) %all-reduce.3.cloned.1.call-update) | async-done | bytes 1048592
  275.0 1.4 constant_dynamic-slice_fusion.2
  276.5 9.5 %all_to_all.62 = bf16[1,4,2,2048]{3,2,0,1:T(2,128)(2,1)S(1)} all-to-all(bf16[1,4,2,2048]{3,2,0,1:T(2,128)(2,1)S(1)} %copy.59), channel_id=1, replica_groups=mesh['narrow'=4,'wide'=32] {'narrow'}, dimensions={1} | all-to-all | bytes 65536 | tf_op jit(solution)/shard_map/all_to_all | solution.py:139
  286.0 0.6 copy.89
  (36 shorter events, 1.1 us)
Async XLA Ops:
  6.5 165.0 %copy-start = (bf16[256,2048]{1,0:T(8,128)(2,1)S(1)}, bf16[256,2048]{1,0:T(8,128)(2,1)}, u32[]{:S(2)}) copy-start(bf16[256,2048]{1,0:T(8,128)(2,1)} %param.12) | copy-start | bytes 3145732
  6.5 53.6 %all-gather.4.cloned.1.call-start = ((), (), s32[]{:S(2)}) async-start(), calls=%async_computation.6 | async-start | bytes 1081344 | tf_op jit(solution)/shard_map/all_gather | solution.py:106
  16.8 68.2 %reduce-scatter.2.cloned.1.call-start = ((), (), s32[]{:S(2)}) async-start(), calls=%async_computation.5 | async-start | bytes 491520 | tf_op jit(solution)/shard_map/reduce_scatter | solution.py:110
  63.5 1.3 copy-start.1
  86.5 14.7 %all-to-all-start.1 = ((bf16[32,2,1,320]{3,1,2,0:T(2,128)(2,1)}), bf16[32,2,1,320]{3,1,2,0:T(2,128)(2,1)S(1)}, u32[]{:S(2)}, u32[]{:S(2)}) async-start(bf16[32,2,1,320]{3,1,2,0:T(2,128)(2,1)} %copy.52), calls=%async_computation.2 | async-start | bytes 98304 | tf_op jit(solution)/shard_map/all_to_all | solution.py:112
  93.8 181.3 %all-reduce.3.cloned.1.call-start = ((), (), s32[]{:S(2)}) async-start(), calls=%async_computation.7 | async-start | bytes 2097152
  172.0 1.9 copy-start.2
Sparse Core Ops, SparseCore 0:
  16.9 43.2 all-gather.3
  64.9 20.0 reduce-scatter.1
  174.0 100.9 all-reduce.2
where the time goes:
time: 295 us; the launch traced here: 293 us
  waiting for transfers between devices  169 us (57%)
  blocking collectives  77.3 us (26%)
  local copies, waits for them, and re-layouts  19.6 us (7%)
  between operations  14 us (5%)
  starting transfers between devices  7.31 us (2%)
  matrix products  3.54 us (1%)
    unnamed x4, waiting for transfers between devices  101 us
    all_to_all x1, blocking collectives, on_device(): lax.all_to_all(spread, 'wide', split_axis=1, concat_axis=0, tiled=True)  45.6 us
    all_gather x1, waiting for transfers between devices, on_device(): shard_piece = lax.all_gather(local_cols, 'wide', axis=0, tiled=True)  42.1 us
    reduce_scatter x1, waiting for transfers between devices, on_device(): lax.psum_scatter(partial_terms, 'narrow', scatter_dimension=1, tiled=True)  19.6 us
    all_gather x1, blocking collectives, on_device(): gathered = lax.all_gather(blocks, 'narrow', axis=1, tiled=True)  12 us
    all_to_all x1, blocking collectives, on_device(): lax.all_to_all(pieces, 'narrow', split_axis=2, concat_axis=0, tiled=True)  10.2 us
    all_to_all x1, blocking collectives, on_device(): lax.all_to_all(own_rows, 'narrow', split_axis=1, concat_axis=3, tiled=True)  9.53 us
    dynamic_slice x2, local copies, waits for them, and re-layouts, visit(): lax.dynamic_slice_in_dim(value_cache, offset, block_size, 1)  7.47 us
  transfers between devices with their start and end apart: 4, of which 4 were waited for; matrix products, arithmetic and copies ran while one was open for 1% of the time, Pallas kernels for 0%

commit v1 on v0

v1 whole, which is shorter than its diff:
```python
import math

import jax
import jax.numpy as jnp
from jax import lax
from jax.experimental import pallas as pl
from jax.experimental.pallas import tpu as pltpu
from jax.sharding import Mesh
from jax.sharding import PartitionSpec as P

HD = 128
KVH = 8
PER = 8
ROPE_BASE = 500000.0
MASKED = -1e30
BLOCK = 512
MIB = 1024 * 1024

HIDE_WEIGHTS = pl.CostEstimate(flops=6 * 10**9, bytes_accessed=2**20, transcendentals=0)
HIDE_CACHES = pl.CostEstimate(flops=3 * 10**10, bytes_accessed=2**21, transcendentals=0)

CHIPS = ("y", "z", "x")
ALL = ("y", "z", "x", "c")
CORE_FIRST = ("c", "y", "z", "x")

VMEM = pl.BlockSpec(memory_space=pltpu.VMEM)
SMEM = pl.BlockSpec(memory_space=pltpu.SMEM)


def rope_tables(positions):
    half = HD // 2
    frequency = jnp.exp(
        -jnp.log(ROPE_BASE) * jnp.arange(half, dtype=jnp.float32) * 2.0 / HD
    )
    angles = positions.astype(jnp.float32)[:, None] * frequency
    cosine = jnp.cos(angles)
    sine = jnp.sin(angles)
    return (
        jnp.concatenate([cosine, cosine], axis=-1),
        jnp.concatenate([-sine, sine], axis=-1),
    )


def flat(block):
    return block.reshape((block.shape[0] * block.shape[1], block.shape[2]))


def stage_kernel(hidden_ref, o_ref):
    o_ref[...] = hidden_ref[...]


def stage_hidden(hidden):
    return pl.pallas_call(
        stage_kernel,
        out_shape=jax.ShapeDtypeStruct(hidden.shape, hidden.dtype),
        in_specs=[VMEM],
        out_specs=VMEM,
        compiler_params=pltpu.CompilerParams(vmem_limit_bytes=8 * MIB),
        name="stage_hidden",
    )(hidden)


def spread_kernel(hidden_ref, o_ref):
    narrow, plane, _, part = o_ref.shape
    for y in range(narrow):
        piece = hidden_ref[:, y * part : (y + 1) * part]
        for i in range(plane):
            o_ref[y, i] = piece


def spread_hidden(hidden, narrow, plane):
    rows, model = hidden.shape
    return pl.pallas_call(
        spread_kernel,
        out_shape=jax.ShapeDtypeStruct((narrow, plane, rows, model // narrow), hidden.dtype),
        in_specs=[VMEM],
        out_specs=VMEM,
        compiler_params=pltpu.CompilerParams(vmem_limit_bytes=8 * MIB),
        cost_estimate=HIDE_WEIGHTS,
        name="spread_hidden",
    )(hidden)


def multiply(tokens_ref, query_ref, memory_ref):
    tokens = flat(tokens_ref[...])
    queries = jnp.dot(tokens, query_ref[...], preferred_element_type=jnp.float32)
    memory = lax.dot_general(
        tokens,
        memory_ref[...],
        (((1,), (1,)), ((), ())),
        preferred_element_type=jnp.float32,
    )
    return jnp.concatenate([queries.astype(jnp.bfloat16), memory.astype(jnp.bfloat16)], axis=1)


def project_mine_kernel(tokens_ref, query_ref, memory_ref, o_ref):
    o_ref[...] = multiply(tokens_ref, query_ref, memory_ref).reshape(o_ref.shape)


def project_other_kernel(tokens_ref, mine_ref, query_ref, memory_ref, o_ref):
    core = lax.axis_index("c")
    o_ref[core] = mine_ref[...]
    o_ref[1 - core] = multiply(tokens_ref, query_ref, memory_ref).reshape(o_ref.shape[1:])


def project_mine(tokens, query_weight, memory_weight):
    chips, rows, part = tokens.shape
    cols = query_weight.shape[1] + memory_weight.shape[0]
    return pl.pallas_call(
        project_mine_kernel,
        out_shape=jax.ShapeDtypeStruct((chips, rows, cols), jnp.bfloat16),
        in_specs=[VMEM] * 3,
        out_specs=VMEM,
        compiler_params=pltpu.CompilerParams(vmem_limit_bytes=12 * MIB),
        cost_estimate=pl.CostEstimate(flops=10**9, bytes_accessed=2**20, transcendentals=0),
        name="project_mine",
    )(tokens, query_weight, memory_weight)


def project_other(tokens, mine, query_weight, memory_weight):
    return pl.pallas_call(
        project_other_kernel,
        out_shape=jax.ShapeDtypeStruct((2,) + mine.shape, jnp.bfloat16),
        in_specs=[VMEM] * 4,
        out_specs=VMEM,
        compiler_params=pltpu.CompilerParams(vmem_limit_bytes=12 * MIB),
        cost_estimate=HIDE_CACHES,
        name="project_other",
    )(tokens, mine, query_weight, memory_weight)


def attend_kernel(
    lengths_ref, cosine_ref, sine_ref, part_ref, k_ref, v_ref, o_ref,
    sums, queries, fresh_keys, fresh_values, scores, attended, paired,
):
    rows, cache, _ = k_ref.shape
    narrow, plane = part_ref.shape[1:3]
    scale = 1.0 / math.sqrt(HD)
    pair = 2 * PER
    span = plane * rows

    for c in range(2):
        total = flat(part_ref[c, 0]).astype(jnp.float32)
        for y in range(1, narrow):
            total += flat(part_ref[c, y]).astype(jnp.float32)
        total = total.astype(jnp.bfloat16).astype(jnp.float32)
        for j in range(2):
            sums[j, c * span : (c + 1) * span] = total[:, j * HD : (j + 1) * HD]
        sums[2, c * span : (c + 1) * span, : HD // 2] = total[:, 2 * HD :]

    lane = lax.broadcasted_iota(jnp.int32, (KVH, HD), 1) // 32
    for s in range(rows):
        cosine = cosine_ref[s : s + 1]
        sine = sine_ref[s : s + 1]

        def rotate(block):
            return block * cosine + pltpu.roll(block, HD // 2, 1) * sine

        for c in range(2):
            for j in range(2):
                piece = sums[j, pl.ds(c * span + s, plane, stride=rows), :]
                queries[s, pl.ds(2 * c + j, plane, stride=4), :] = rotate(piece)
        key = jnp.zeros((KVH, HD), jnp.float32)
        value = jnp.zeros((KVH, HD), jnp.float32)
        for b in range(2):
            for c in range(2):
                m = 2 * b + c
                piece = sums[2, pl.ds(c * span + b * rows + s, KVH, stride=2 * rows), :]
                key = jnp.where(lane == m, pltpu.roll(piece, 32 * m, 1) if m else piece, key)
                value = jnp.where(
                    lane == m, pltpu.roll(piece, (32 * m - 32) % HD, 1) if m != 1 else piece, value
                )
        fresh_keys[s] = rotate(key).astype(jnp.bfloat16).astype(jnp.float32)
        fresh_values[s] = value

    def spread_groups(block):
        return jnp.concatenate(
            [jnp.broadcast_to(block[g : g + 1], (PER, HD)) for g in range(KVH)], axis=0
        )

    @pl.loop(0, rows)
    def _(s):
        length = lengths_ref[s]
        halves = (length + (BLOCK - 1)) // BLOCK
        whole = halves // 2
        rest = halves - 2 * whole
        q = queries[s].astype(jnp.bfloat16)
        blank = jnp.zeros((PER, HD), jnp.bfloat16)
        wide_q = []
        for t in range(KVH // 2):
            lower = q[t * pair : t * pair + PER]
            upper = q[t * pair + PER : (t + 1) * pair]
            wide_q.append(
                jnp.concatenate(
                    [
                        jnp.concatenate([lower, blank], axis=1),
                        jnp.concatenate([blank, upper], axis=1),
                    ],
                    axis=0,
                )
            )
        own = (
            jnp.sum(q.astype(jnp.float32) * spread_groups(fresh_keys[s]), axis=1, keepdims=True)
            * scale
        )

        def score(start, size, top):
            at = pl.ds(pl.multiple_of(start, BLOCK), size)
            block = (
                jnp.concatenate(
                    [
                        lax.dot_general(
                            wide_q[t],
                            k_ref[s, at, 2 * t * HD : 2 * (t + 1) * HD],
                            (((1,), (1,)), ((), ())),
                            preferred_element_type=jnp.float32,
                        )
                        for t in range(KVH // 2)
                    ],
                    axis=0,
                )
                * scale
            )
            position = start + lax.broadcasted_iota(jnp.int32, block.shape, 1)
            block = jnp.where(position < length, block, MASKED)
            scores[:, at] = block
            return jnp.maximum(top, jnp.max(block, axis=1, keepdims=True))

        top = lax.fori_loop(0, whole, lambda i, c: score(2 * i * BLOCK, 2 * BLOCK, c), own)
        top = lax.fori_loop(0, rest, lambda i, c: score(2 * whole * BLOCK, BLOCK, c), top)
        own_exp = jnp.exp(own - top)

        def mix(start, size, carry):
            total, mixed = carry
            at = pl.ds(pl.multiple_of(start, BLOCK), size)
            exps = jnp.exp(scores[:, at] - top)
            weights = exps.astype(jnp.bfloat16)
            parts = []
            for t in range(KVH // 2):
                both = jnp.dot(
                    weights[t * pair : (t + 1) * pair],
                    v_ref[s, at, 2 * t * HD : 2 * (t + 1) * HD],
                    preferred_element_type=jnp.float32,
                )
                parts += [both[:PER, :HD], both[PER:, HD:]]
            return (
                total + jnp.sum(exps, axis=1, keepdims=True),
                mixed + jnp.concatenate(parts, axis=0),
            )

        carry = (
            own_exp,
            own_exp.astype(jnp.bfloat16).astype(jnp.float32) * spread_groups(fresh_values[s]),
        )
        carry = lax.fori_loop(0, whole, lambda i, c: mix(2 * i * BLOCK, 2 * BLOCK, c), carry)
        total, mixed = lax.fori_loop(0, rest, lambda i, c: mix(2 * whole * BLOCK, BLOCK, c), carry)
        attended[s] = mixed / total

    for s in range(rows):
        for h in range(4):
            paired[h, pl.ds(s, plane, stride=rows), :] = attended[
                s, pl.ds(h, plane, stride=4), :
            ]
    block = jnp.concatenate([paired[h] for h in range(4)], axis=1).astype(jnp.bfloat16)
    block = block.reshape(o_ref.shape[1:])
    for y in range(narrow):
        o_ref[y] = block


def attend(partial, cosine, sine, key_cache, value_cache, lengths):
    _, narrow, plane, rows, cols = partial.shape
    cache, width = key_cache.shape[1:]
    heads = 4 * plane
    return pl.pallas_call(
        attend_kernel,
        out_shape=jax.ShapeDtypeStruct((narrow, plane, rows, 4 * HD), jnp.bfloat16),
        in_specs=[SMEM] + [VMEM] * 5,
        out_specs=VMEM,
        scratch_shapes=[
            pltpu.VMEM((3, 2 * plane * rows, HD), jnp.float32),
            pltpu.VMEM((rows, heads, HD), jnp.float32),
            pltpu.VMEM((rows, KVH, HD), jnp.float32),
            pltpu.VMEM((rows, KVH, HD), jnp.float32),
            pltpu.VMEM((heads, cache), jnp.float32),
            pltpu.VMEM((rows, heads, HD), jnp.float32),
            pltpu.VMEM((4, plane * rows, HD), jnp.float32),
        ],
        compiler_params=pltpu.CompilerParams(vmem_limit_bytes=24 * MIB),
        cost_estimate=pl.CostEstimate(
            flops=8 * rows * heads * cache * HD,
            bytes_accessed=4 * rows * cache * width,
            transcendentals=rows * heads * cache,
        ),
        name="attend",
    )(lengths, cosine, sine, partial, key_cache, value_cache)


def output_kernel(tokens_ref, weight_ref, other_ref, o_ref):
    core = lax.axis_index("c")
    heads = weight_ref.shape[0]

    def half(owner, ref):
        at = pl.ds(pl.multiple_of(owner * heads, heads), heads)
        return jnp.dot(
            flat(tokens_ref[:, :, at]), ref[...], preferred_element_type=jnp.float32
        )

    total = half(core, weight_ref) + half(1 - core, other_ref)
    o_ref[...] = total.astype(jnp.bfloat16).reshape(o_ref.shape)


def output(tokens, weight, other):
    chips, rows, _ = tokens.shape
    return pl.pallas_call(
        output_kernel,
        out_shape=jax.ShapeDtypeStruct((chips, rows, weight.shape[1]), jnp.bfloat16),
        in_specs=[VMEM] * 3,
        out_specs=VMEM,
        compiler_params=pltpu.CompilerParams(vmem_limit_bytes=12 * MIB),
        name="output",
    )(tokens, weight, other)


def gather_sums_kernel(parts_ref, o_ref):
    narrow, plane, rows, part = parts_ref.shape
    span = plane * rows
    pick = lax.broadcasted_iota(jnp.int32, (PER, span), 1) % rows
    pick = (pick == lax.broadcasted_iota(jnp.int32, (PER, span), 0)).astype(jnp.bfloat16)
    for y in range(narrow):
        total = jnp.dot(pick, flat(parts_ref[y]), preferred_element_type=jnp.float32)
        o_ref[:, y * part : (y + 1) * part] = total[:rows].astype(o_ref.dtype)


def gather_sums(parts):
    narrow, plane, rows, part = parts.shape
    return pl.pallas_call(
        gather_sums_kernel,
        out_shape=jax.ShapeDtypeStruct((rows, narrow * part), jnp.bfloat16),
        in_specs=[VMEM],
        out_specs=VMEM,
        compiler_params=pltpu.CompilerParams(vmem_limit_bytes=8 * MIB),
        name="gather_sums",
    )(parts)


def on_device(
    hidden_state, query_weight, memory_weight, output_weight, key_cache, value_cache, cache_lengths
):
    narrow = lax.axis_size("y")
    plane = lax.axis_size("z") * lax.axis_size("x")
    chips = narrow * plane
    swap = [(0, 1), (1, 0)]
    rows, model = hidden_state.shape
    part = model // narrow
    query_cols = query_weight.shape[1]
    cols = query_cols + 2 * memory_weight.shape[2]
    heads_local = output_weight.shape[0]

    pieces = spread_hidden(stage_hidden(hidden_state), narrow, plane).reshape(chips, rows, part)
    mine = lax.all_to_all(pieces, CHIPS, split_axis=0, concat_axis=0, tiled=True)
    mine, lengths = lax.optimization_barrier((mine, cache_lengths))
    other = lax.ppermute(mine, "c", swap)
    tables = rope_tables(lengths)
    memory_weight = memory_weight.transpose(1, 2, 0).reshape(-1, part)
    from_mine = project_mine(mine, query_weight, memory_weight)
    other, from_mine, cosine, sine, own_output = lax.optimization_barrier(
        (other, from_mine, *tables, output_weight)
    )
    other_output = lax.ppermute(own_output, "c", swap)

    partial = project_other(other, from_mine, query_weight, memory_weight)
    partial = lax.all_to_all(
        partial.reshape(2 * chips, rows, cols), CORE_FIRST, split_axis=0, concat_axis=0, tiled=True
    )

    spread = attend(
        partial.reshape(2, narrow, plane, rows, cols),
        cosine,
        sine,
        key_cache,
        value_cache,
        lengths,
    )
    spread, other_output = lax.optimization_barrier((spread, other_output))

    gathered = lax.all_to_all(
        spread.reshape(chips, rows, 2 * heads_local),
        CHIPS,
        split_axis=0,
        concat_axis=0,
        tiled=True,
    )
    summed = output(gathered, own_output, other_output)
    returned = lax.all_to_all(summed, CHIPS, split_axis=0, concat_axis=0, tiled=True)
    return gather_sums(returned.reshape(narrow, plane, rows, part))


def solution(mesh):
    count = mesh.devices.size
    narrow = mesh.shape["narrow"]
    side = math.isqrt(mesh.shape["wide"] // 2)
    split = Mesh(mesh.devices.reshape(narrow, side, count // (2 * narrow * side), 2), ALL)
    wide = ("z", "x", "c")
    in_specs = (
        P(ALL, None),
        P("y", wide),
        P("y", None, wide),
        P(wide, "y"),
        P(ALL, None, None),
        P(ALL, None, None),
        P(ALL),
    )
    return jax.shard_map(
        on_device, mesh=split, in_specs=in_specs, out_specs=P(ALL, None), check_vma=False
    )
```

time: 295 us -> 80.3 us (0.27)
  waiting for transfers between devices: 169 us -> 1.23 us
  local copies, waits for them, and re-layouts: 19.6 us -> 0.79 us
  between operations: 14 us -> 0.14 us
  starting transfers between devices: 7.31 us -> 0.22 us
  Pallas kernels: 0 us -> 5.83 us
  blocking collectives: 77.3 us -> 71.8 us
  matrix products: 3.54 us -> 0 us
    unnamed x4 -> x0, waiting for transfers between devices: 101 us -> none
    all_gather x1 -> x0, waiting for transfers between devices: 42.1 us -> none  [on_device(): shard_piece = lax.all_gather(local_cols, 'wide', axis=0, tiled=True)]
    reduce_scatter x1 -> x0, waiting for transfers between devices: 19.6 us -> none  [on_device(): lax.psum_scatter(partial_terms, 'narrow', scatter_dimension=1, tiled=True)]
    all_gather x1 -> x0, blocking collectives: 12 us -> none  [on_device(): gathered = lax.all_gather(blocks, 'narrow', axis=1, tiled=True)]
    dynamic_slice x3 -> x0, local copies, waits for them, and re-layouts: 10.3 us -> none  [the longest x2 7.47 us: visit(): lax.dynamic_slice_in_dim(value_cache, offset, block_size, 1)]
    all_to_all x1 -> x0, starting transfers between devices: 7.23 us -> none  [on_device(): lax.all_to_all(projected, 'wide', split_axis=0, concat_axis=2, tiled=True)]
    all_to_all x1 -> x0, waiting for transfers between devices: 6.61 us -> none  [on_device(): lax.all_to_all(projected, 'wide', split_axis=0, concat_axis=2, tiled=True)]
    all_to_all x3 -> x4, blocking collectives: 65.3 us -> 71.8 us  [the longest x1 24.9 us: on_device(): lax.all_to_all(pieces, CHIPS, split_axis=0, concat_axis=0, tiled=True)]
  transfers between devices with their start and end apart: 4 -> 2, of which waited for: 4 -> 1; matrix products, arithmetic and copies ran while one was open for 1% -> 0% of each run, Pallas kernels for 0% -> 6%
where the time goes in v1:
time: 80.3 us; the launch traced here: 80.2 us
  blocking collectives  71.8 us (89%)
  Pallas kernels  5.83 us (7%)
  waiting for transfers between devices  1.23 us (2%)
    all_to_all x1, blocking collectives, on_device(): lax.all_to_all(pieces, CHIPS, split_axis=0, concat_axis=0, tiled=True)  24.9 us
    all_to_all x1, blocking collectives, on_device(): lax.all_to_all(summed, CHIPS, split_axis=0, concat_axis=0, tiled=True)  17.5 us
    all_to_all x1, blocking collectives, on_device(): lax.all_to_all(spread.reshape(chips, rows, 2 * heads_local), CHIPS, split...  15.2 us
    all_to_all x1, blocking collectives, on_device(): lax.all_to_all(partial.reshape(2 * chips, rows, cols), CORE_FIRST, split_...  14.1 us
    pallas_call x1, Pallas kernels, attend(): pl.pallas_call(attend_kernel, out_shape=jax.ShapeDtypeStruct((narrow, pla...  3.63 us
  transfers between devices with their start and end apart: 2, of which 1 were waited for; matrix products, arithmetic and copies ran while one was open for 0% of the time, Pallas kernels for 6%

profile of v1, /device:TPU:0, one launch (start us, length us, event | category | flops | bytes accessed | tf_op | source)
XLA Modules:
  0.0 80.2 jit_solution(16617563578794090800)
XLA Ops:
  0.0 0.0 copy-start.1
  0.0 0.8 copy-done.1
  0.8 0.0 copy-start.2
  0.8 0.0 copy-start.3
  0.8 0.0 copy-start.4
  0.8 0.0 copy-start
  0.8 24.9 %all_to_all.20.tokens_ref = bf16[64,2,2048]{2,1,0:T(2,128)(2,1)S(1)} all-to-all(bf16[64,2,2048]{2,1,0:T(2,128)(2,1)S(1)} %bitcast.15), channel_id=1, replica_groups=mesh['y'=4,'z'=4,'x'=4,'c'=2] {'y','z','x'}, dimensions={0} | all-to-all | bytes 1048576 | tf_op jit(solution)/shard_map/all_to_all | solution.py:360
  25.7 0.0 collective-permute-start
  25.7 0.0 copy-done.2
  25.7 0.0 copy-done.3
  25.8 0.0 copy-done.4
  25.8 0.4 project_mine.1.mine_ref
  26.2 0.1 fusion
  26.3 0.1 pad_maximum_fusion
  26.4 1.2 %collective-permute-done.tokens_ref = bf16[64,2,2048]{2,1,0:T(2,128)(2,1)S(1)} collective-permute-done((bf16[64,2,2048]{2,1,0:T(2,128)(2,1)S(1)}, bf16[64,2,2048]{2,1,0:T(2,128)(2,1)S(1)}, u32[]{:S(2)}, u32[]{:S(2)}) %collective-permute-start) | collective-permute-done | bytes 524320 | tf_op jit(solution)/shard_map/ppermute | solution.py:362
  27.6 0.0 slice-start
  27.6 0.0 slice-start.2
  27.6 0.0 copy-done
  27.6 0.0 slice-start.3
  27.6 0.2 collective-permute-start.1
  27.9 0.4 project_other.1
  28.3 14.1 %all_to_all.21 = bf16[128,2,320]{2,1,0:T(2,128)(2,1)S(1)} all-to-all(bf16[128,2,320]{2,1,0:T(2,128)(2,1)S(1)} %bitcast.16), channel_id=1, replica_groups=mesh['y'=4,'z'=4,'x'=4,'c'=2] {'c','y','z','x'}, dimensions={0} | all-to-all | bytes 327680 | tf_op jit(solution)/shard_map/all_to_all | solution.py:372
  42.4 0.0 slice-done
  42.4 0.0 slice-done.2
  42.4 0.0 slice-done.1
  42.4 0.0 slice-done.3
  42.5 3.6 %attend.1 = bf16[4,16,2,512]{3,2,1,0:T(2,128)(2,1)S(1)} custom-call(s32[2]{0:T(128)S(1)} %copy-done.2, f32[2,128]{1,0:T(2,128)S(1)} %get-tuple-element.16.cosine_ref, f32[2,128]{1,0:T(2,128)S(1)} %get-tuple-element.17.sine_ref, bf16[2,4,16,2,320]{4,3,2,1,0:T(2,128)(2,1)S(1)} %bitcast.13, bf16[2,2048,1024]{2,1,0:T(8,128)(2,1)S(1)} %bitcast.9, ...), custom_call_target="tpu_custom_call" | custom-call | flops 268435456 | bytes 16777216 | tf_op jit(solution)/shard_map/attend/pallas_call | solution.py:274
  46.1 0.0 collective-permute-done.1.other_ref
  46.1 15.2 %all_to_all.22.tokens_ref = bf16[64,2,512]{2,1,0:T(2,128)(2,1)S(1)} all-to-all(bf16[64,2,512]{2,1,0:T(2,128)(2,1)S(1)} %bitcast.14), channel_id=1, replica_groups=mesh['y'=4,'z'=4,'x'=4,'c'=2] {'y','z','x'}, dimensions={0} | all-to-all | bytes 262144 | tf_op jit(solution)/shard_map/all_to_all | solution.py:386
  61.3 0.5 output.1
  61.8 17.5 %all_to_all.23 = bf16[64,2,2048]{2,1,0:T(2,128)(2,1)S(1)} all-to-all(bf16[64,2,2048]{2,1,0:T(2,128)(2,1)S(1)} %output.1), channel_id=1, replica_groups=mesh['y'=4,'z'=4,'x'=4,'c'=2] {'y','z','x'}, dimensions={0} | all-to-all | bytes 1048576 | tf_op jit(solution)/shard_map/all_to_all | solution.py:394
  79.3 0.8 %gather_sums.1 = bf16[2,8192]{1,0:T(2,128)(2,1)} custom-call(bf16[4,16,2,2048]{3,2,1,0:T(2,128)(2,1)S(1)} %bitcast.12), custom_call_target="tpu_custom_call" | custom-call | tf_op jit(solution)/shard_map/gather_sums/pallas_call | solution.py:336
  (7 shorter events, 0.1 us)
Async XLA Ops:
  0.0 0.8 copy-start.1
  0.8 25.0 %copy-start.2 = (s32[2]{0:T(128)S(1)}, s32[2]{0:T(128)}, u32[]{:S(2)}) copy-start(s32[2]{0:T(128)} %lengths_ref) | copy-start | bytes 28
  0.8 25.0 %copy-start.3 = (bf16[2048,256]{1,0:T(8,128)(2,1)S(1)}, bf16[2048,256]{1,0:T(8,128)(2,1)}, u32[]{:S(2)}) copy-start(bf16[2048,256]{1,0:T(8,128)(2,1)} %query_ref.3) | copy-start | bytes 3145732
  0.8 25.0 %copy-start.4 = (bf16[2048,2,32]{0,2,1:T(8,128)(2,1)S(1)}, bf16[2048,2,32]{0,2,1:T(8,128)(2,1)}, u32[]{:S(2)}) copy-start(bf16[2048,2,32]{0,2,1:T(8,128)(2,1)} %param.9) | copy-start | bytes 786436
  0.8 26.9 %copy-start = (bf16[256,2048]{1,0:T(8,128)(2,1)S(1)}, bf16[256,2048]{1,0:T(8,128)(2,1)}, u32[]{:S(2)}) copy-start(bf16[256,2048]{1,0:T(8,128)(2,1)} %weight_ref) | copy-start | bytes 3145732
  25.7 1.9 %collective-permute-start = (bf16[64,2,2048]{2,1,0:T(2,128)(2,1)S(1)}, bf16[64,2,2048]{2,1,0:T(2,128)(2,1)S(1)}, u32[]{:S(2)}, u32[]{:S(2)}) collective-permute-start(bf16[64,2,2048]{2,1,0:T(2,128)(2,1)S(1)} %all_to_all.20.tokens_ref), channel_id=1, source_target_pairs={{0,1},{1,0},{2,3},{3,2},{4,5},{5,4},{6,7},{7,6},{8,9},{9,8},{10,11... | collective-permute-start | bytes 1572872 | tf_op jit(solution)/shard_map/ppermute | solution.py:362
  27.6 14.8 %slice-start = ((s8[8388608]{0:T(1024)(128)(4,1)}), s8[4194304]{0:T(1024)(128)(4,1)S(1)}, s32[]{:S(2)}) async-start(s8[8388608]{0:T(1024)(128)(4,1)} %bitcast.8), calls=%async_computation.4 | async-start | bytes 8388608
  27.6 14.8 %slice-start.2 = ((s8[8388608]{0:T(1024)(128)(4,1)}), s8[4194304]{0:T(1024)(128)(4,1)S(1)}, s32[]{:S(2)}) async-start(s8[8388608]{0:T(1024)(128)(4,1)} %bitcast.10), calls=%async_computation.6 | async-start | bytes 8388608
  27.6 14.8 %slice-start.1 = ((s8[8388608]{0:T(1024)(128)(4,1)}), s8[4194304]{0:T(1024)(128)(4,1)S(1)}, s32[]{:S(2)}) async-start(s8[8388608]{0:T(1024)(128)(4,1)} %bitcast.8), calls=%async_computation.5 | async-start | bytes 8388608
  27.6 14.8 %slice-start.3 = ((s8[8388608]{0:T(1024)(128)(4,1)}), s8[4194304]{0:T(1024)(128)(4,1)S(1)}, s32[]{:S(2)}) async-start(s8[8388608]{0:T(1024)(128)(4,1)} %bitcast.10), calls=%async_computation.7 | async-start | bytes 8388608
  27.6 18.5 %collective-permute-start.1 = (bf16[256,2048]{1,0:T(8,128)(2,1)S(1)}, bf16[256,2048]{1,0:T(8,128)(2,1)S(1)}, u32[]{:S(2)}, u32[]{:S(2)}) collective-permute-start(bf16[256,2048]{1,0:T(8,128)(2,1)S(1)} %copy-done), channel_id=1, source_target_pairs={{0,1},{1,0},{2,3},{3,2},{4,5},{5,4},{6,7},{7,6},{8,9},{9,8},{10,11... | collective-permute-start | bytes 3145736 | tf_op jit(solution)/shard_map/ppermute | solution.py:369
